TPU v7x, 256 devices: a whole 4x4x8 slice. The times are simulated.
256 devices in a mesh: band: 64 (over y, z, x_lo), grid: 4 (over x_hi, core).
Axes of the slice: x: 4 (x_hi: 2, x_lo: 2; x = x_hi * 2 + x_lo), y: 4, z: 8, core: 2. Of those that a mesh axis runs over, the one named last changes fastest.
Arguments:
- orbitals: bfloat16 [256, 48, 2304], P('band', 'grid'), may hold values from -6 to 6
Outputs:
- exchange: float32 [256, 48, 2304], P('band', 'grid')
All inputs are finite; a program needn't handle non-finite values.
Results may differ from a plain program's by a relative error of at most 0.0003.
Values may be sent and summed in bfloat16 or wider, within the bound.
A program may use at most 64 MiB of HBM per device.

v0:
```python
import math

import jax
import jax.numpy as jnp
import ml_dtypes
import numpy as np
from jax import lax
from jax.experimental import pallas as pl
from jax.experimental.pallas import tpu as pltpu
from jax.sharding import PartitionSpec as P

POINTS = 48
PLANE = POINTS * POINTS
GROUP = 4
SLAB = 12
BAND = 64
CHUNK = 384
BOX = 37.25
OMEGA = 0.106
MIXING = 0.25
ROWS = 4 * GROUP * SLAB
CLASSES = ((0, 384), (384, 384), (768, 768), (1536, 768))


def halves(table):
    high = table.astype(ml_dtypes.bfloat16)
    low = (table - high.astype(np.float64)).astype(ml_dtypes.bfloat16)
    return high, low


def tables():
    index = np.arange(POINTS)
    angles = 2.0 * np.pi * (np.outer(index, index) % POINTS) / POINTS
    cas = np.cos(angles) + np.sin(angles)

    def spread(weights):
        rows = np.zeros((8, POINTS))
        for fine in range(8):
            rows[fine, fine::8] = weights
        return rows

    even, odd = [1, 1, 1, 1, 1, 1], [1, -1, 1, -1, 1, -1]
    real2, imag2 = [1, -0.5, -0.5, 1, -0.5, -0.5], [0, 1, -1, 0, 1, -1]
    real1, imag1 = [1, 0.5, -0.5, -1, -0.5, 0.5], [0, 1, 1, 0, -1, -1]
    matrices, order = [], []
    for parts, residues in (
        ((even,), (0,)),
        ((odd,), (3,)),
        ((real2, imag2), (2, 4)),
        ((real1, imag1), (1, 5)),
    ):
        folded = np.concatenate([spread(part) for part in parts])
        waves = [k for k in range(POINTS) if k % 6 in residues]
        small = cas[waves] @ folded.T @ np.linalg.inv(folded @ folded.T)
        matrices.append(np.kron(small, cas))
        order += waves
    signed = ((index + POINTS // 2) % POINTS - POINTS // 2) * (2.0 * np.pi / BOX)
    along_y, along_z = np.repeat(np.array(order), POINTS), np.tile(index, POINTS)
    squares = (
        signed[:, None] ** 2 + signed[along_y][None] ** 2 + signed[along_z][None] ** 2
    )
    bounded = np.where(squares > 0.0, squares, 1.0)
    screened = 4.0 * np.pi / bounded * (1.0 - np.exp(-bounded / (4.0 * OMEGA * OMEGA)))
    screened = np.where(squares > 0.0, screened, np.pi / (OMEGA * OMEGA)) / POINTS**3

    forward = [halves(m.T) for m in matrices]
    inverse = [halves(m) for m in matrices]
    small = np.stack([np.stack([w[c][p] for c in (0, 1) for p in (0, 1)]) for w in (forward, inverse)])
    large = np.stack([np.stack([w[c][p] for c in (2, 3) for p in (0, 1)]) for w in (forward, inverse)])

    first, second = [], []
    for device in range(4):
        matrix = np.zeros((GROUP, POINTS, 4, GROUP, SLAB))
        for slot in range(4):
            base = SLAB * (device ^ slot)
            for orbital in range(GROUP):
                matrix[orbital, :, slot, orbital, :] = cas[:, base : base + SLAB]
        matrix = matrix.reshape(ROWS, ROWS)
        for source, out in ((matrix, first), (matrix.T, second)):
            high, low = halves(source)
            out.append(np.concatenate([high, low, high], axis=1))
    along_x = np.stack([np.stack(first), np.stack(second)], axis=1)
    return small, large, along_x, screened.astype(np.float32)


def parted(value):
    high = value.astype(jnp.bfloat16)
    return high, (value - high.astype(jnp.float32)).astype(jnp.bfloat16)


def dot(left, right):
    return jnp.dot(left, right, preferred_element_type=jnp.float32)


def fold(d):
    s = [d[p] + d[p + 3] for p in range(3)]
    t = [d[p] - d[p + 3] for p in range(3)]
    u, v = s[1] + s[2], t[1] - t[2]
    return (s[0] + u, t[0] - v, s[0] - 0.5 * u, s[1] - s[2], t[0] + 0.5 * v, t[1] + t[2])


def unfold(f):
    z0, z3, r2, i2, r1, i1 = f
    a, b = z0 - 0.5 * r2, z3 - 0.5 * r1
    s = (z0 + r2, a + i2, a - i2)
    t = (z3 + r1, i1 - b, i1 + b)
    return [s[p] + t[p] for p in range(3)] + [s[p] - t[p] for p in range(3)]


def densities(slots, home_in, wide, z_hi, z_lo):
    for q in slots:
        for r in range(0, POINTS, 16):
            for tile in range(3):
                d = []
                for p in range(6):
                    lanes = pl.ds(p * CHUNK + tile * 128, 128)
                    rows = pl.ds(r, 16)
                    d.append(home_in[q, rows, lanes].astype(jnp.float32) * wide[q, rows, lanes])
                for p, value in enumerate(fold(d)):
                    high, low = parted(value)
                    at = (pl.ds(q * POINTS + r, 16), pl.ds(p * CHUNK + tile * 128, 128))
                    z_hi[at] = high
                    z_lo[at] = low


def weights(small, large, which, cls):
    return (small, large)[cls // 2], which, 2 * (cls % 2)


def plane(rows, cls, source, table):
    high, low = source
    ref, which, base = table
    first, lanes = CLASSES[cls]
    at = (pl.ds(rows[0], rows[1]), pl.ds(first, lanes))
    left = jnp.concatenate([high[at], high[at], low[at]], axis=1)
    w_hi, w_lo = ref[which, base], ref[which, base + 1]
    return dot(left, jnp.concatenate([w_hi, w_lo, w_hi], axis=0))


def middle(cls, s, u, along_x, screened):
    first, lanes = CLASSES[cls]
    for start in range(first, first + lanes, CHUNK):
        at = (slice(None), pl.ds(start, CHUNK))
        s_hi, s_lo = s[0][at], s[1][at]
        spectrum = dot(along_x[0], jnp.concatenate([s_hi, s_hi, s_lo], axis=0))
        table = screened[at]
        weighted = spectrum * jnp.concatenate([table] * GROUP, axis=0)
        t_hi, t_lo = parted(weighted)
        back = dot(along_x[1], jnp.concatenate([t_hi, t_hi, t_lo], axis=0))
        u[0][at], u[1][at] = parted(back)


def products(q, last, home_in, wide, g, home_sum, vis_sum):
    for tile in range(3):
        f = []
        for p in range(6):
            f.append(g[pl.ds(q * POINTS, POINTS), pl.ds(p * CHUNK + tile * 128, 128)])
        for p, value in enumerate(unfold(f)):
            column = p * CHUNK + tile * 128
            lanes = pl.ds(column, 128)
            home = value * wide[q, :, lanes]
            if last:
                home = home + home_sum[q, :, lanes]
            home_sum[q, :, lanes] = home
            other = value * home_in[q, :, lanes].astype(jnp.float32)
            other = other[:24] + other[24:]
            other = other[:SLAB] + other[SLAB:]
            half = column // 1152
            vis_sum[q, pl.ds(SLAB * half, SLAB), pl.ds(column - 1152 * half, 128)] = other


def kernel(
    orbitals, packed, small_hbm, large_hbm, along_hbm, screened_hbm, out,
    home_in, vis_in, wide, z_hi, z_lo, s_hi, s_lo, g,
    home_sum, vis_sum, sib_relay, sib_final, far_out, far_in, vis_back,
    small, large, along_x, screened,
    table_sem, own_sem, home_send, home_recv, vis_send, vis_recv,
    sum_send, sum_recv, back_send, back_recv,
):
    band, me = lax.axis_index("band"), lax.axis_index("grid")

    def partner(bit):
        return me + bit - 2 * bit * (lax.rem(me // bit, 2))

    def group(distance):
        return lax.rem(band + distance + BAND, BAND)

    sibling, far = (band, partner(1)), (band, partner(2))

    barrier = pltpu.get_barrier_semaphore()
    pl.semaphore_signal(barrier, 1, device_id=sibling)
    pl.semaphore_signal(barrier, 1, device_id=far)
    for distance in (-2, -1, 1, 2):
        for j in range(4):
            pl.semaphore_signal(barrier, 1, device_id=(group(distance), j))

    own = pltpu.make_async_copy(packed, home_in.at[0], own_sem)
    own.start()
    loads = [
        pltpu.make_async_copy(small_hbm, small, table_sem.at[0]),
        pltpu.make_async_copy(large_hbm, large, table_sem.at[1]),
        pltpu.make_async_copy(along_hbm.at[me], along_x, table_sem.at[2]),
        pltpu.make_async_copy(screened_hbm, screened, table_sem.at[3]),
    ]
    for load in loads:
        load.start()
    pl.semaphore_wait(barrier, 18)

    def home_copy(source, slot, target):
        return pltpu.make_async_remote_copy(
            source, home_in.at[slot], home_send.at[slot], home_recv.at[slot], device_id=target
        )

    def xor(a, j):
        low = lax.rem(a + j, 2)
        high = lax.rem(a // 2 + j // 2, 2)
        return 2 * high + low

    far_copy = home_copy(packed, 2, far)
    far_copy.start()
    sib_copy = home_copy(packed, 1, sibling)
    sib_copy.start()
    vis_copies = []
    for s in (1, 0):
        for j in range(4):
            copy = pltpu.make_async_remote_copy(
                orbitals.at[j],
                vis_in.at[s, xor(me, j)],
                vis_send.at[s, j],
                vis_recv.at[s, xor(me, j)],
                device_id=(group(s + 1), j),
            )
            copy.start()
            vis_copies.append(copy)

    def widen(s, slots):
        for q in slots:
            pltpu.make_async_remote_copy(
                orbitals.at[0], vis_in.at[s, q], vis_send.at[s, 0], vis_recv.at[s, q],
                device_id=sibling,
            ).wait_recv()
            value = vis_in[s, q].astype(jnp.float32)
            for i in range(GROUP):
                wide[s, q, pl.ds(SLAB * i, SLAB), :] = value

    def forward(s, rows):
        for cls in range(4):
            first, lanes = CLASSES[cls]
            value = plane(rows, cls, (z_hi, z_lo), weights(small, large, 0, cls))
            at = (pl.ds(rows[0], rows[1]), pl.ds(first, lanes))
            s_hi[at], s_lo[at] = parted(value)

    def backward(rows):
        for cls in range(4):
            first, lanes = CLASSES[cls]
            value = plane(rows, cls, (s_hi, s_lo), weights(small, large, 1, cls))
            g[pl.ds(rows[0], rows[1]), pl.ds(first, lanes)] = value

    own.wait()
    sib_copy.wait_recv()
    widen(1, (0, 1))
    densities((0, 1), home_in, wide.at[1], z_hi, z_lo)
    for load in loads:
        load.wait()
    forward(1, (0, 96))
    far_copy.wait_recv()
    relay = home_copy(home_in.at[2], 3, sibling)
    relay.start()
    widen(1, (2, 3))
    densities((2,), home_in, wide.at[1], z_hi, z_lo)
    relay.wait_recv()
    densities((3,), home_in, wide.at[1], z_hi, z_lo)
    forward(1, (96, 96))
    for cls in range(4):
        middle(cls, (s_hi, s_lo), (s_hi, s_lo), along_x, screened)
    backward((0, ROWS))
    for q in range(4):
        products(q, False, home_in, wide.at[1], g, home_sum, vis_sum.at[1])

    def send_back(s, q):
        copy = pltpu.make_async_remote_copy(
            vis_sum.at[s, q],
            vis_back.at[s, me],
            back_send.at[s, q],
            back_recv.at[s, me],
            device_id=(group(-s - 1), xor(me, q)),
        )
        copy.start()
        return copy

    back_copies = [send_back(1, q) for q in range(4)]

    widen(0, range(4))
    densities(range(4), home_in, wide.at[0], z_hi, z_lo)
    forward(0, (0, ROWS))
    for cls in range(4):
        middle(cls, (s_hi, s_lo), (s_hi, s_lo), along_x, screened)

    def sum_copy(source, target_ref, slot, target):
        return pltpu.make_async_remote_copy(
            source, target_ref, sum_send.at[slot], sum_recv.at[slot], device_id=target
        )

    backward((96, 96))
    products(3, True, home_in, wide.at[0], g, home_sum, vis_sum.at[0])
    to_relay = sum_copy(home_sum.at[3], sib_relay, 0, sibling)
    to_relay.start()
    products(2, True, home_in, wide.at[0], g, home_sum, vis_sum.at[0])
    back_copies += [send_back(0, 3), send_back(0, 2)]
    to_relay.wait_recv()
    far_out[...] = home_sum[2] + sib_relay[...]
    to_far = sum_copy(far_out, far_in, 1, far)
    to_far.start()
    backward((0, 96))
    products(1, True, home_in, wide.at[0], g, home_sum, vis_sum.at[0])
    to_final = sum_copy(home_sum.at[1], sib_final, 2, sibling)
    to_final.start()
    products(0, True, home_in, wide.at[0], g, home_sum, vis_sum.at[0])
    back_copies += [send_back(0, 1), send_back(0, 0)]

    to_final.wait_recv()
    for s in (1, 0):
        for j in range(4):
            pltpu.make_async_remote_copy(
                vis_sum.at[s, 0], vis_back.at[s, j], back_send.at[s, 0], back_recv.at[s, j],
                device_id=sibling,
            ).wait_recv()
    to_far.wait_recv()
    for i in range(GROUP):
        rows = pl.ds(SLAB * i, SLAB)
        for half in range(2):
            lanes = pl.ds(1152 * half, 1152)
            part = pl.ds(SLAB * half, SLAB)
            total = home_sum[0, rows, lanes] + sib_final[rows, lanes] + far_in[rows, lanes]
            total = total + (vis_back[0, i, part, :] + vis_back[1, i, part, :])
            out[i, :, lanes] = -MIXING * total

    for copy in [far_copy, sib_copy, relay, to_relay, to_far, to_final] + vis_copies + back_copies:
        copy.wait_send()


def solution(mesh):
    small, large, along_x, screened = tables()
    any_space = pl.BlockSpec(memory_space=pl.ANY)
    bf16, f32 = jnp.bfloat16, jnp.float32
    dma = pltpu.SemaphoreType.DMA
    call = pl.pallas_call(
        kernel,
        out_shape=jax.ShapeDtypeStruct((GROUP, SLAB, PLANE), f32),
        in_specs=[any_space] * 6,
        out_specs=pl.BlockSpec(memory_space=pltpu.VMEM),
        scratch_shapes=[
            pltpu.VMEM((4, POINTS, PLANE), bf16),
            pltpu.VMEM((2, 4, SLAB, PLANE), bf16),
            pltpu.VMEM((2, 4, POINTS, PLANE), f32),
            pltpu.VMEM((ROWS, PLANE), bf16),
            pltpu.VMEM((ROWS, PLANE), bf16),
            pltpu.VMEM((ROWS, PLANE), bf16),
            pltpu.VMEM((ROWS, PLANE), bf16),
            pltpu.VMEM((ROWS, PLANE), f32),
            pltpu.VMEM((4, POINTS, PLANE), f32),
            pltpu.VMEM((2, 4, 24, PLANE // 2), f32),
            pltpu.VMEM((POINTS, PLANE), f32),
            pltpu.VMEM((POINTS, PLANE), f32),
            pltpu.VMEM((POINTS, PLANE), f32),
            pltpu.VMEM((POINTS, PLANE), f32),
            pltpu.VMEM((2, 4, 24, PLANE // 2), f32),
            pltpu.VMEM(small.shape, bf16),
            pltpu.VMEM(large.shape, bf16),
            pltpu.VMEM(along_x.shape[1:], bf16),
            pltpu.VMEM(screened.shape, f32),
            dma((4,)), dma, dma((4,)), dma((4,)), dma((2, 4)), dma((2, 4)),
            dma((3,)), dma((3,)), dma((2, 4)), dma((2, 4)),
        ],
        compiler_params=pltpu.CompilerParams(
            collective_id=0, has_side_effects=True, vmem_limit_bytes=60 << 20
        ),
    )

    def body(orbitals):
        packed = orbitals.reshape(GROUP * SLAB, PLANE)
        return call(orbitals, packed, small, large, along_x, screened)

    placed = P("band", "grid", None)
    return jax.shard_map(
        body, mesh=mesh, in_specs=(placed,), out_specs=placed, check_vma=False
    )
```

profile of v0, /device:TPU:1, one launch (start us, length us, event | category | flops | bytes accessed | tf_op | source)
XLA Modules:
  0.0 63.0 jit_solution(12466390824781184645)
XLA Ops:
  0.0 1.0 %copy.10.orbitals = bf16[4,12,2304]{2,1,0:T(8,128)(2,1)S(1)} copy(bf16[4,12,2304]{2,0,1:T(4,128)(2,1)} %param.5) | data formatting | bytes 442368 | tf_op args[0]
  1.0 0.0 copy-start
  1.0 0.8 %reshape.3.packed = bf16[48,2304]{1,0:T(8,128)(2,1)} reshape(bf16[4,12,2304]{2,1,0:T(8,128)(2,1)S(1)} %copy.10.orbitals) | data formatting | bytes 442368 | tf_op jit(solution)/shard_map/reshape | solution.py:381
  1.8 0.0 copy-done
  1.8 59.1 %shard_map.55 = f32[4,12,2304]{2,1,0:T(8,128)} custom-call(bf16[4,12,2304]{2,1,0:T(8,128)(2,1)} %copy-done, bf16[48,2304]{1,0:T(8,128)(2,1)} %reshape.3.packed, bf16[2,4,384,384]{3,2,1,0:T(8,128)(2,1)} %constant.8.clone.small_hbm, bf16[2,4,768,768]{3,2,1,0:T(8,128)(2,1)} %constant.9.clone.large_hbm, bf16[4,2,192,576]{3,2,1,0:T(8,128)(2,1)} %constant.10.clone.along_hbm, ...), custom_call_target="tpu_custom_call" | custom-call | tf_op jit(solution)/shard_map/pallas_call | solution.py:382
  60.9 2.1 %copy.11 = f32[4,12,2304]{2,0,1:T(4,128)} copy(f32[4,12,2304]{2,1,0:T(8,128)} %shard_map.55) | data formatting | bytes 884736 | tf_op jit(solution)/shard_map/pallas_call | solution.py:382
Async XLA Ops:
  1.0 0.8 %copy-start = (bf16[4,12,2304]{2,1,0:T(8,128)(2,1)}, bf16[4,12,2304]{2,1,0:T(8,128)(2,1)S(1)}, u32[]{:S(2)}) copy-start(bf16[4,12,2304]{2,1,0:T(8,128)(2,1)S(1)} %copy.10.orbitals) | copy-start | bytes 663556
where the time goes:
time: 63.3 us; the launch traced here: 63 us
  Pallas kernels  59.1 us (93%)
  local copies, waits for them, and re-layouts  3.86 us (6%)
    pallas_call x1, Pallas kernels, body(): return call(orbitals, packed, small, large, along_x, screened)  59.1 us
    pallas_call x1, local copies, waits for them, and re-layouts, body(): return call(orbitals, packed, small, large, along_x, screened)  2.11 us

commit v1 on v0

v1 whole, which is shorter than its diff:
```python
import functools

import jax
import jax.numpy as jnp
import ml_dtypes
import numpy as np
from jax import lax
from jax.experimental import pallas as pl
from jax.experimental.pallas import tpu as pltpu
from jax.sharding import PartitionSpec as P

POINTS = 48
PLANE = POINTS * POINTS
GROUP = 4
SLAB = 12
BAND = 64
CHUNK = 384
BOX = 37.25
OMEGA = 0.106
MIXING = 0.25
ROWS = 4 * GROUP * SLAB
HALF = ROWS // 2
CLASSES = ((0, 384), (384, 384), (768, 768), (1536, 768))


def halves(table):
    high = table.astype(ml_dtypes.bfloat16)
    low = (table - high.astype(np.float64)).astype(ml_dtypes.bfloat16)
    return high, low


def tables():
    index = np.arange(POINTS)
    angles = 2.0 * np.pi * (np.outer(index, index) % POINTS) / POINTS
    cas = np.cos(angles) + np.sin(angles)

    def spread(weights):
        rows = np.zeros((8, POINTS))
        for fine in range(8):
            rows[fine, fine::8] = weights
        return rows

    even, odd = [1, 1, 1, 1, 1, 1], [1, -1, 1, -1, 1, -1]
    real2, imag2 = [1, -0.5, -0.5, 1, -0.5, -0.5], [0, 1, -1, 0, 1, -1]
    real1, imag1 = [1, 0.5, -0.5, -1, -0.5, 0.5], [0, 1, 1, 0, -1, -1]
    matrices, order = [], []
    for parts, residues in (
        ((even,), (0,)),
        ((odd,), (3,)),
        ((real2, imag2), (2, 4)),
        ((real1, imag1), (1, 5)),
    ):
        folded = np.concatenate([spread(part) for part in parts])
        waves = [k for k in range(POINTS) if k % 6 in residues]
        small = cas[waves] @ folded.T @ np.linalg.inv(folded @ folded.T)
        matrices.append(np.kron(small, cas))
        order += waves
    signed = ((index + POINTS // 2) % POINTS - POINTS // 2) * (2.0 * np.pi / BOX)
    along_y, along_z = np.repeat(np.array(order), POINTS), np.tile(index, POINTS)
    squares = (
        signed[:, None] ** 2 + signed[along_y][None] ** 2 + signed[along_z][None] ** 2
    )
    bounded = np.where(squares > 0.0, squares, 1.0)
    screened = 4.0 * np.pi / bounded * (1.0 - np.exp(-bounded / (4.0 * OMEGA * OMEGA)))
    screened = np.where(squares > 0.0, screened, np.pi / (OMEGA * OMEGA)) / POINTS**3

    forward = [halves(m.T) for m in matrices]
    inverse = [halves(m) for m in matrices]
    small = np.stack([np.stack([w[c][p] for c in (0, 1) for p in (0, 1)]) for w in (forward, inverse)])
    large = np.stack([np.stack([w[c][p] for c in (2, 3) for p in (0, 1)]) for w in (forward, inverse)])

    along = []
    for device in range(4):
        matrix = np.zeros((2, POINTS, 4, 2, SLAB))
        for slot in range(4):
            base = SLAB * (device ^ slot)
            for orbital in range(2):
                matrix[orbital, :, slot, orbital, :] = cas[:, base : base + SLAB]
        matrix = matrix.reshape(HALF, HALF)
        for source in (matrix, matrix.T):
            high, low = halves(source)
            top = np.concatenate([high, high], axis=1)
            bottom = np.concatenate([low, np.zeros_like(low)], axis=1)
            along.append(np.concatenate([top, bottom], axis=0))
    along_x = np.stack(along).reshape(4, 2, ROWS, ROWS)
    return small, large, along_x, screened.astype(np.float32)


def parted(value):
    high = value.astype(jnp.bfloat16)
    return high, (value - high.astype(jnp.float32)).astype(jnp.bfloat16)


def dot(left, right):
    return jnp.dot(left, right, preferred_element_type=jnp.float32)


def fold(d):
    s = [d[p] + d[p + 3] for p in range(3)]
    t = [d[p] - d[p + 3] for p in range(3)]
    u, v = s[1] + s[2], t[1] - t[2]
    return (s[0] + u, t[0] - v, s[0] - 0.5 * u, s[1] - s[2], t[0] + 0.5 * v, t[1] + t[2])


def unfold(f):
    z0, z3, r2, i2, r1, i1 = f
    a, b = z0 - 0.5 * r2, z3 - 0.5 * r1
    s = (z0 + r2, a + i2, a - i2)
    t = (z3 + r1, i1 - b, i1 + b)
    return [s[p] + t[p] for p in range(3)] + [s[p] - t[p] for p in range(3)]


def densities(pair, home_in, wide, z_hi, z_lo):
    for tile in range(3):
        d = []
        for p in range(6):
            lanes = pl.ds(p * CHUNK + tile * 128, 128)
            d.append([home_in[2 * pair + k, :, lanes].astype(jnp.float32) * wide[2 * pair + k, :, lanes] for k in range(2)])
        for two in range(2):
            rows = slice(24 * two, 24 * two + 24)
            parts = [jnp.concatenate([value[rows] for value in values], axis=0) for values in d]
            for p, value in enumerate(fold(parts)):
                at = (pl.ds(HALF * two + POINTS * pair, POINTS), pl.ds(p * CHUNK + tile * 128, 128))
                z_hi[at], z_lo[at] = parted(value)


def weights(small, large, which, cls):
    return (small, large)[cls // 2], which, 2 * (cls % 2)


def segments(pairs):
    return [HALF * two + POINTS * pair for two in range(2) for pair in pairs]


def plane(pairs, cls, source, table):
    ref, which, base = table
    first, lanes = CLASSES[cls]
    high, low = (
        jnp.concatenate([part[pl.ds(row, POINTS), pl.ds(first, lanes)] for row in segments(pairs)], axis=0)
        for part in source
    )
    count = high.shape[0]
    both = dot(jnp.concatenate([high, low], axis=0), ref[which, base])
    return both[:count] + both[count:] + dot(high, ref[which, base + 1])


def middle(start, s, u, along_x, screened):
    lanes = pl.ds(start, 768)
    table = screened[:, lanes]
    for two in range(2):
        at = (pl.ds(HALF * two, HALF), lanes)
        both = dot(along_x[0], jnp.concatenate([s[0][at], s[1][at]], axis=0))
        weighted = (both[:HALF] + both[HALF:]) * jnp.concatenate([table] * 2, axis=0)
        both = dot(along_x[1], jnp.concatenate(parted(weighted), axis=0))
        u[0][at], u[1][at] = parted(both[:HALF] + both[HALF:])


def products(q, last, home_in, wide, g, home_sum, vis_sum):
    for tile in range(3):
        f = []
        for p in range(6):
            lanes = pl.ds(p * CHUNK + tile * 128, 128)
            f.append(jnp.concatenate([g[pl.ds(HALF * two + 24 * q, 24), lanes] for two in range(2)], axis=0))
        for p, value in enumerate(unfold(f)):
            column = p * CHUNK + tile * 128
            lanes = pl.ds(column, 128)
            home = value * wide[q, :, lanes]
            if last:
                home = home + home_sum[q, :, lanes]
            home_sum[q, :, lanes] = home
            other = value * home_in[q, :, lanes].astype(jnp.float32)
            other = other[:24] + other[24:]
            other = other[:SLAB] + other[SLAB:]
            part, place = divmod(column // 128, 5)
            vis_sum[q, pl.ds(SLAB * part, SLAB), pl.ds(128 * place, 128)] = other


def scale_of(values):
    top = functools.reduce(jnp.maximum, [jnp.max(jnp.abs(v), axis=0, keepdims=True) for v in values])
    top = jnp.max(top, axis=1, keepdims=True)
    return (220.0 / jnp.maximum(top, 1e-30)).astype(jnp.bfloat16).astype(jnp.float32)


def coded(value, scale):
    power = value * scale
    for _ in range(4):
        power = power * power
    return jnp.where(value < 0.0, -power, power).astype(jnp.bfloat16)


def decoded(code, inverse):
    power = code.astype(jnp.float32)
    value = jnp.exp2(jnp.log2(jnp.abs(power)) * 0.0625) * inverse
    return jnp.where(power < 0.0, -value, value)


def code_visitor(source, target):
    tiles = [source[:, pl.ds(128 * k, 128)] for k in range(5)]
    scale = scale_of(tiles)
    spare = lax.broadcasted_iota(jnp.int32, (POINTS, 128), 0) >= 3 * SLAB
    for k in range(5):
        code = coded(tiles[k], scale)
        if k >= 3:
            code = jnp.where(spare, jnp.broadcast_to(scale, (POINTS, 128)), code.astype(jnp.float32))
        target[:, pl.ds(128 * k, 128)] = code.astype(jnp.bfloat16)


def kernel(
    arrived, small_hbm, large_hbm, along_hbm, screened_hbm, out,
    spread_rows, orbitals, home_in, vis_in, wide, z_hi, z_lo, s_hi, s_lo, g,
    home_sum, vis_sum, vis_code, sib_relay, sib_final, far_sum, far_out, far_in, vis_back,
    small, large, along_x, screened,
    table_sem, home_send, home_recv, vis_send, vis_recv,
    sum_send, sum_recv, back_send, back_recv,
):
    band, me = lax.axis_index("band"), lax.axis_index("grid")

    def partner(bit):
        return me + bit - 2 * bit * (lax.rem(me // bit, 2))

    def group(distance):
        return lax.rem(band + distance + BAND, BAND)

    sibling, far = (band, partner(1)), (band, partner(2))

    barrier = pltpu.get_barrier_semaphore()
    pl.semaphore_signal(barrier, 1, device_id=sibling)
    pl.semaphore_signal(barrier, 1, device_id=far)
    for distance in (-2, -1, 1, 2):
        for j in range(4):
            pl.semaphore_signal(barrier, 1, device_id=(group(distance), j))

    loads = [
        pltpu.make_async_copy(small_hbm, small, table_sem.at[0]),
        pltpu.make_async_copy(large_hbm, large, table_sem.at[1]),
        pltpu.make_async_copy(along_hbm.at[me], along_x, table_sem.at[2]),
        pltpu.make_async_copy(screened_hbm, screened, table_sem.at[3]),
    ]
    for load in loads:
        load.start()
    for k in range(18):
        lanes = pl.ds(128 * k, 128)
        for r in range(SLAB):
            spread_rows[k, pl.ds(r, GROUP, stride=SLAB), :] = arrived[r, :, lanes].astype(jnp.float32)
        home_in[0, :, lanes] = spread_rows[k].astype(jnp.bfloat16)
        for i in range(GROUP):
            orbitals[i, :, lanes] = spread_rows[k, pl.ds(SLAB * i, SLAB), :].astype(jnp.bfloat16)
    vis_sum[...] = jnp.zeros_like(vis_sum)
    pl.semaphore_wait(barrier, 18)

    def home_copy(source, slot, target):
        return pltpu.make_async_remote_copy(
            source, home_in.at[slot], home_send.at[slot], home_recv.at[slot], device_id=target
        )

    def xor(a, j):
        low = lax.rem(a + j, 2)
        high = lax.rem(a // 2 + j // 2, 2)
        return 2 * high + low

    far_copy = home_copy(home_in.at[0], 2, far)
    far_copy.start()
    sib_copy = home_copy(home_in.at[0], 1, sibling)
    sib_copy.start()
    vis_copies = []

    def send_visitors(s):
        for j in range(4):
            copy = pltpu.make_async_remote_copy(
                orbitals.at[j],
                vis_in.at[s, xor(me, j)],
                vis_send.at[s, j],
                vis_recv.at[s, xor(me, j)],
                device_id=(group(s + 1), j),
            )
            copy.start()
            vis_copies.append(copy)

    send_visitors(1)

    def widen(s, slots):
        for q in slots:
            pltpu.make_async_remote_copy(
                orbitals.at[0], vis_in.at[s, q], vis_send.at[s, 0], vis_recv.at[s, q],
                device_id=sibling,
            ).wait_recv()
            value = vis_in[s, q].astype(jnp.float32)
            for i in range(GROUP):
                wide[s, q, pl.ds(SLAB * i, SLAB), :] = value

    def forward(pairs):
        for cls in range(4):
            first, lanes = CLASSES[cls]
            value = plane(pairs, cls, (z_hi, z_lo), weights(small, large, 0, cls))
            for k, row in enumerate(segments(pairs)):
                at = (pl.ds(row, POINTS), pl.ds(first, lanes))
                s_hi[at], s_lo[at] = parted(value[POINTS * k : POINTS * k + POINTS])

    def backward(pairs):
        for cls in range(4):
            first, lanes = CLASSES[cls]
            value = plane(pairs, cls, (s_hi, s_lo), weights(small, large, 1, cls))
            for k, row in enumerate(segments(pairs)):
                g[pl.ds(row, POINTS), pl.ds(first, lanes)] = value[POINTS * k : POINTS * k + POINTS]

    def across():
        for start in range(0, PLANE, 768):
            middle(start, (s_hi, s_lo), (s_hi, s_lo), along_x, screened)

    sib_copy.wait_recv()
    widen(1, (0, 1))
    densities(0, home_in, wide.at[1], z_hi, z_lo)
    for load in loads:
        load.wait()
    forward((0,))
    far_copy.wait_recv()
    relay = home_copy(home_in.at[2], 3, sibling)
    relay.start()
    widen(1, (2, 3))
    send_visitors(0)
    relay.wait_recv()
    densities(1, home_in, wide.at[1], z_hi, z_lo)
    forward((1,))
    across()
    backward((0, 1))
    for q in range(4):
        products(q, False, home_in, wide.at[1], g, home_sum, vis_sum.at[1])

    def send_back(s, q):
        code_visitor(vis_sum.at[s, q], vis_code.at[s, q])
        copy = pltpu.make_async_remote_copy(
            vis_code.at[s, q],
            vis_back.at[s, me],
            back_send.at[s, q],
            back_recv.at[s, me],
            device_id=(group(-s - 1), xor(me, q)),
        )
        copy.start()
        return copy

    back_copies = [send_back(1, q) for q in range(4)]

    widen(0, range(4))
    densities(0, home_in, wide.at[0], z_hi, z_lo)
    densities(1, home_in, wide.at[0], z_hi, z_lo)
    forward((0, 1))
    across()

    def sum_copy(source, target_ref, slot, target):
        return pltpu.make_async_remote_copy(
            source, target_ref, sum_send.at[slot], sum_recv.at[slot], device_id=target
        )

    backward((1,))
    products(3, True, home_in, wide.at[0], g, home_sum, vis_sum.at[0])
    to_relay = sum_copy(home_sum.at[3], sib_relay, 0, sibling)
    to_relay.start()
    products(2, True, home_in, wide.at[0], g, home_sum, vis_sum.at[0])
    back_copies += [send_back(0, 3), send_back(0, 2)]
    to_relay.wait_recv()
    columns = [pl.ds(128 * k, 128) for k in range(18)]
    for lanes in columns:
        far_sum[:, lanes] = home_sum[2, :, lanes] + sib_relay[:, lanes]
    scale = scale_of([far_sum[:, lanes] for lanes in columns])
    for lanes in columns:
        far_out[:, lanes] = coded(far_sum[:, lanes], scale)
    far_out[:, pl.ds(PLANE, 128)] = jnp.broadcast_to(scale, (POINTS, 128)).astype(jnp.bfloat16)
    to_far = sum_copy(far_out, far_in, 1, far)
    to_far.start()
    backward((0,))
    products(1, True, home_in, wide.at[0], g, home_sum, vis_sum.at[0])
    to_final = sum_copy(home_sum.at[1], sib_final, 2, sibling)
    to_final.start()
    products(0, True, home_in, wide.at[0], g, home_sum, vis_sum.at[0])
    back_copies += [send_back(0, 1), send_back(0, 0)]

    to_final.wait_recv()
    for s in (1, 0):
        for j in range(4):
            pltpu.make_async_remote_copy(
                vis_code.at[s, 0], vis_back.at[s, j], back_send.at[s, 0], back_recv.at[s, j],
                device_id=sibling,
            ).wait_recv()
    to_far.wait_recv()
    far_inverse = 1.0 / far_in[pl.ds(0, 16), pl.ds(PLANE, 128)].astype(jnp.float32)[:1]
    vis_inverse = [
        [1.0 / vis_back[s, i, pl.ds(32, 16), pl.ds(384, 128)].astype(jnp.float32)[15:] for i in range(4)]
        for s in range(2)
    ]
    for k in range(18):
        lanes = pl.ds(128 * k, 128)
        total = home_sum[0, :, lanes] + sib_final[:, lanes] + decoded(far_in[:, lanes], far_inverse)
        part, place = divmod(k, 5)
        for i in range(GROUP):
            values = [
                decoded(vis_back[s, i, :, pl.ds(128 * place, 128)], vis_inverse[s][i])
                for s in range(2)
            ]
            back = values[0] + values[1]
            mine = total[SLAB * i : SLAB * i + SLAB] + back[SLAB * part : SLAB * part + SLAB]
            out[:, i, lanes] = mine

    for copy in [far_copy, sib_copy, relay, to_relay, to_far, to_final] + vis_copies + back_copies:
        copy.wait_send()


def solution(mesh):
    small, large, along_x, screened = tables()
    any_space = pl.BlockSpec(memory_space=pl.ANY)
    bf16, f32 = jnp.bfloat16, jnp.float32
    dma = pltpu.SemaphoreType.DMA
    call = pl.pallas_call(
        kernel,
        out_shape=jax.ShapeDtypeStruct((SLAB, GROUP, PLANE), f32),
        in_specs=[pl.BlockSpec(memory_space=pltpu.VMEM)] + [any_space] * 4,
        out_specs=pl.BlockSpec(memory_space=pltpu.VMEM),
        scratch_shapes=[
            pltpu.VMEM((18, POINTS, 128), f32),
            pltpu.VMEM((GROUP, SLAB, PLANE), bf16),
            pltpu.VMEM((4, POINTS, PLANE), bf16),
            pltpu.VMEM((2, 4, SLAB, PLANE), bf16),
            pltpu.VMEM((2, 4, POINTS, PLANE), f32),
            pltpu.VMEM((ROWS, PLANE), bf16),
            pltpu.VMEM((ROWS, PLANE), bf16),
            pltpu.VMEM((ROWS, PLANE), bf16),
            pltpu.VMEM((ROWS, PLANE), bf16),
            pltpu.VMEM((ROWS, PLANE), f32),
            pltpu.VMEM((4, POINTS, PLANE), f32),
            pltpu.VMEM((2, 4, POINTS, 640), f32),
            pltpu.VMEM((2, 4, POINTS, 640), bf16),
            pltpu.VMEM((POINTS, PLANE), f32),
            pltpu.VMEM((POINTS, PLANE), f32),
            pltpu.VMEM((POINTS, PLANE), f32),
            pltpu.VMEM((POINTS, PLANE + 128), bf16),
            pltpu.VMEM((POINTS, PLANE + 128), bf16),
            pltpu.VMEM((2, 4, POINTS, 640), bf16),
            pltpu.VMEM(small.shape, bf16),
            pltpu.VMEM(large.shape, bf16),
            pltpu.VMEM(along_x.shape[1:], bf16),
            pltpu.VMEM(screened.shape, f32),
            dma((4,)), dma((4,)), dma((4,)), dma((2, 4)), dma((2, 4)),
            dma((3,)), dma((3,)), dma((2, 4)), dma((2, 4)),
        ],
        compiler_params=pltpu.CompilerParams(
            collective_id=0, has_side_effects=True, vmem_limit_bytes=60 << 20
        ),
    )

    def body(orbitals):
        return -MIXING * jnp.transpose(
            call(jnp.transpose(orbitals, (1, 0, 2)), small, large, along_x, screened), (1, 0, 2)
        )

    placed = P("band", "grid", None)
    return jax.shard_map(
        body, mesh=mesh, in_specs=(placed,), out_specs=placed, check_vma=False
    )
```

time: 63.3 us -> 53.1 us (0.84)
  Pallas kernels: 59.1 us -> 50.7 us
  local copies, waits for them, and re-layouts: 3.86 us -> 0 us
  other arithmetic: 0 us -> 1.87 us
    pallas_call x1, Pallas kernels: 59.1 us -> 50.7 us  [body(): call(jnp.transpose(orbitals, (1, 0, 2)), small, large, along_x, screened)]
    pallas_call x1 -> x0, local copies, waits for them, and re-layouts: 2.11 us -> none  [body(): return call(orbitals, packed, small, large, along_x, screened)]
    mul x0 -> x1, other arithmetic: none -> 1.87 us  [body(): -MIXING]
    unnamed x3 -> x0, local copies, waits for them, and re-layouts: 0.97 us -> none
    reshape x1 -> x0, local copies, waits for them, and re-layouts: 0.77 us -> none  [body(): packed = orbitals.reshape(GROUP * SLAB, PLANE)]
where the time goes in v1:
time: 53.1 us; the launch traced here: 52.6 us
  Pallas kernels  50.7 us (95%)
  other arithmetic  1.87 us (4%)
    pallas_call x1, Pallas kernels, body(): call(jnp.transpose(orbitals, (1, 0, 2)), small, large, along_x, screened)  50.7 us
    mul x1, other arithmetic, body(): -MIXING  1.87 us

profile of v1, /device:TPU:1, one launch (start us, length us, event | category | flops | bytes accessed | tf_op | source)
XLA Modules:
  0.0 52.6 jit_solution(8423318838329657442)
XLA Ops:
  0.0 50.7 %shard_map.55 = f32[12,4,2304]{2,1,0:T(4,128)} custom-call(bf16[12,4,2304]{2,1,0:T(4,128)(2,1)} %bitcast.3, bf16[2,4,384,384]{3,2,1,0:T(8,128)(2,1)} %constant.10.clone.small_hbm, bf16[2,4,768,768]{3,2,1,0:T(8,128)(2,1)} %constant.11.clone.large_hbm, bf16[4,2,192,192]{3,2,1,0:T(8,128)(2,1)} %constant.12.clone.along_hbm, f32[48,2304]{1,0:T(8,128)} %constant.13.clone.screened_hbm), custom_call_target="tpu_custom_call" | custom-call | tf_op jit(solution)/shard_map/pallas_call | solution.py:451
  50.7 1.9 %multiply_bitcast_fusion = f32[4,12,2304]{2,0,1:T(4,128)} fusion(f32[12,4,2304]{2,1,0:T(4,128)} %shard_map.55), kind=kLoop, calls=%fused_computation | loop fusion | flops 110592 | bytes 884736 | tf_op jit(solution)/shard_map/mul | solution.py:450

commit v2 on v1

v2 whole, which is shorter than its diff:
```python
import functools

import jax
import jax.numpy as jnp
import ml_dtypes
import numpy as np
from jax import lax
from jax.experimental import pallas as pl
from jax.experimental.pallas import tpu as pltpu
from jax.sharding import PartitionSpec as P

POINTS = 48
PLANE = POINTS * POINTS
GROUP = 4
SLAB = 12
BAND = 64
CHUNK = 384
BOX = 37.25
OMEGA = 0.106
MIXING = 0.25
ROWS = 4 * GROUP * SLAB
HALF = ROWS // 2
BEHIND = (-1, 2)
CLASSES = ((0, 384), (384, 384), (768, 768), (1536, 768))


def halves(table):
    high = table.astype(ml_dtypes.bfloat16)
    low = (table - high.astype(np.float64)).astype(ml_dtypes.bfloat16)
    return high, low


def tables():
    index = np.arange(POINTS)
    angles = 2.0 * np.pi * (np.outer(index, index) % POINTS) / POINTS
    cas = np.cos(angles) + np.sin(angles)

    def spread(weights):
        rows = np.zeros((8, POINTS))
        for fine in range(8):
            rows[fine, fine::8] = weights
        return rows

    even, odd = [1, 1, 1, 1, 1, 1], [1, -1, 1, -1, 1, -1]
    real2, imag2 = [1, -0.5, -0.5, 1, -0.5, -0.5], [0, 1, -1, 0, 1, -1]
    real1, imag1 = [1, 0.5, -0.5, -1, -0.5, 0.5], [0, 1, 1, 0, -1, -1]
    matrices, order = [], []
    for parts, residues in (
        ((even,), (0,)),
        ((odd,), (3,)),
        ((real2, imag2), (2, 4)),
        ((real1, imag1), (1, 5)),
    ):
        folded = np.concatenate([spread(part) for part in parts])
        waves = [k for k in range(POINTS) if k % 6 in residues]
        small = cas[waves] @ folded.T @ np.linalg.inv(folded @ folded.T)
        matrices.append(np.kron(small, cas))
        order += waves
    signed = ((index + POINTS // 2) % POINTS - POINTS // 2) * (2.0 * np.pi / BOX)
    along_y, along_z = np.repeat(np.array(order), POINTS), np.tile(index, POINTS)
    squares = (
        signed[:, None] ** 2 + signed[along_y][None] ** 2 + signed[along_z][None] ** 2
    )
    bounded = np.where(squares > 0.0, squares, 1.0)
    screened = 4.0 * np.pi / bounded * (1.0 - np.exp(-bounded / (4.0 * OMEGA * OMEGA)))
    screened = np.where(squares > 0.0, screened, np.pi / (OMEGA * OMEGA)) / POINTS**3

    forward = [halves(m.T) for m in matrices]
    inverse = [halves(m) for m in matrices]
    small = np.stack([np.stack([w[c][p] for c in (0, 1) for p in (0, 1)]) for w in (forward, inverse)])
    large = np.stack([np.stack([w[c][p] for c in (2, 3) for p in (0, 1)]) for w in (forward, inverse)])

    along = []
    for device in range(4):
        matrix = np.zeros((2, POINTS, 4, 2, SLAB))
        for slot in range(4):
            base = SLAB * (device ^ slot)
            for orbital in range(2):
                matrix[orbital, :, slot, orbital, :] = cas[:, base : base + SLAB]
        matrix = matrix.reshape(HALF, HALF)
        for source in (matrix, matrix.T):
            high, low = halves(source)
            top = np.concatenate([high, high], axis=1)
            bottom = np.concatenate([low, np.zeros_like(low)], axis=1)
            along.append(np.concatenate([top, bottom], axis=0))
    along_x = np.stack(along).reshape(4, 2, ROWS, ROWS)
    return small, large, along_x, screened.astype(np.float32)


def parted(value):
    high = value.astype(jnp.bfloat16)
    return high, (value - high.astype(jnp.float32)).astype(jnp.bfloat16)


def dot(left, right):
    return jnp.dot(left, right, preferred_element_type=jnp.float32)


def fold(d):
    s = [d[p] + d[p + 3] for p in range(3)]
    t = [d[p] - d[p + 3] for p in range(3)]
    u, v = s[1] + s[2], t[1] - t[2]
    return (s[0] + u, t[0] - v, s[0] - 0.5 * u, s[1] - s[2], t[0] + 0.5 * v, t[1] + t[2])


def unfold(f):
    z0, z3, r2, i2, r1, i1 = f
    a, b = z0 - 0.5 * r2, z3 - 0.5 * r1
    s = (z0 + r2, a + i2, a - i2)
    t = (z3 + r1, i1 - b, i1 + b)
    return [s[p] + t[p] for p in range(3)] + [s[p] - t[p] for p in range(3)]


def densities(pair, two, home_in, wide, z_hi, z_lo):
    for tile in range(3):
        d = [None] * 6
        for p in range(3):
            lanes = pl.ds(p * CHUNK + tile * 128, 128)
            values = [
                home_in[2 * pair + k, two, :, lanes].astype(jnp.float32) * wide[2 * pair + k, :, lanes]
                for k in range(2)
            ]
            d[p] = jnp.concatenate([value[:24] for value in values], axis=0)
            d[p + 3] = jnp.concatenate([value[24:] for value in values], axis=0)
        for p, value in enumerate(fold(d)):
            at = (pl.ds(HALF * two + POINTS * pair, POINTS), pl.ds(p * CHUNK + tile * 128, 128))
            z_hi[at], z_lo[at] = parted(value)


def weights(small, large, which, cls):
    return (small, large)[cls // 2], which, 2 * (cls % 2)


def plane(two, cls, source, table):
    ref, which, base = table
    first, lanes = CLASSES[cls]
    high, low = (part[pl.ds(HALF * two, HALF), pl.ds(first, lanes)] for part in source)
    both = dot(jnp.concatenate([high, low], axis=0), ref[which, base])
    return both[:HALF] + both[HALF:] + dot(high, ref[which, base + 1])


def middle(start, two, s, u, along_x, screened):
    at = (pl.ds(HALF * two, HALF), pl.ds(start, 768))
    table = screened[:, pl.ds(start, 768)]
    both = dot(along_x[0], jnp.concatenate([s[0][at], s[1][at]], axis=0))
    weighted = (both[:HALF] + both[HALF:]) * jnp.concatenate([table] * 2, axis=0)
    both = dot(along_x[1], jnp.concatenate(parted(weighted), axis=0))
    u[0][at], u[1][at] = parted(both[:HALF] + both[HALF:])


def products(q, two, last, home_in, wide, g, home_sum, vis_part, vis_sum):
    for tile in range(3):
        f = [g[pl.ds(HALF * two + 24 * q, 24), pl.ds(p * CHUNK + tile * 128, 128)] for p in range(6)]
        values = unfold(f)
        for p in range(3):
            lanes = pl.ds(p * CHUNK + tile * 128, 128)
            value = jnp.concatenate([values[p], values[p + 3]], axis=0)
            home = value * wide[q, :, lanes]
            if last:
                home = home + home_sum[q, two, :, lanes]
            home_sum[q, two, :, lanes] = home
            other = value * home_in[q, two, :, lanes].astype(jnp.float32)
            if two == 0:
                vis_part[q, :, lanes] = other
                continue
            other = other + vis_part[q, :, lanes]
            for half in range(2):
                rows = other[24 * half : 24 * half + SLAB] + other[24 * half + SLAB : 24 * half + 24]
                part, place = divmod(9 * half + 3 * p + tile, 5)
                vis_sum[q, pl.ds(SLAB * part, SLAB), pl.ds(128 * place, 128)] = rows


def scale_of(values):
    top = functools.reduce(jnp.maximum, [jnp.max(jnp.abs(v), axis=0, keepdims=True) for v in values])
    top = jnp.max(top, axis=1, keepdims=True)
    return (220.0 / jnp.maximum(top, 1e-30)).astype(jnp.bfloat16).astype(jnp.float32)


def coded(value, scale):
    power = value * scale
    for _ in range(4):
        power = power * power
    return jnp.where(value < 0.0, -power, power).astype(jnp.bfloat16)


def decoded(code, inverse):
    power = code.astype(jnp.float32)
    value = jnp.exp2(jnp.log2(jnp.abs(power)) * 0.0625) * inverse
    return jnp.where(power < 0.0, -value, value)


def code_visitor(source, target):
    tiles = [source[:, pl.ds(128 * k, 128)] for k in range(5)]
    scale = scale_of(tiles)
    spare = lax.broadcasted_iota(jnp.int32, (POINTS, 128), 0) >= 3 * SLAB
    for k in range(5):
        code = coded(tiles[k], scale)
        if k >= 3:
            code = jnp.where(spare, jnp.broadcast_to(scale, (POINTS, 128)), code.astype(jnp.float32))
        target[:, pl.ds(128 * k, 128)] = code.astype(jnp.bfloat16)


def kernel(
    arrived, small_hbm, large_hbm, along_hbm, screened_hbm, out,
    spread_rows, spread_parts, orbitals, home_in, vis_in, wide, z_hi, z_lo, s_hi, s_lo, g,
    home_sum, vis_part, vis_sum, vis_code, sib_relay, sib_final, far_sum, far_out, far_in, vis_back,
    small, large, along_x, screened,
    table_sem, home_send, home_recv, vis_send, vis_recv,
    sum_send, sum_recv, back_send, back_recv,
):
    band, me = lax.axis_index("band"), lax.axis_index("grid")

    def partner(bit):
        return me + bit - 2 * bit * (lax.rem(me // bit, 2))

    def group(distance):
        return lax.rem(band + distance + BAND, BAND)

    def xor(a, j):
        low = lax.rem(a + j, 2)
        high = lax.rem(a // 2 + j // 2, 2)
        return 2 * high + low

    sibling, far = (band, partner(1)), (band, partner(2))

    barrier = pltpu.get_barrier_semaphore()
    pl.semaphore_signal(barrier, 1, device_id=sibling)
    pl.semaphore_signal(barrier, 1, device_id=far)
    for distance in BEHIND:
        for j in range(4):
            pl.semaphore_signal(barrier, 1, device_id=(group(-distance), j))

    loads = [
        pltpu.make_async_copy(small_hbm, small, table_sem.at[0]),
        pltpu.make_async_copy(large_hbm, large, table_sem.at[1]),
        pltpu.make_async_copy(along_hbm.at[me], along_x, table_sem.at[2]),
        pltpu.make_async_copy(screened_hbm, screened, table_sem.at[3]),
    ]
    spread_parts[3:5] = jnp.zeros((2, ROWS, 128), jnp.float32)
    for k in range(18):
        part, place = divmod(k, 5)
        for r in range(SLAB):
            value = arrived[r, :, pl.ds(128 * k, 128)].astype(jnp.float32)
            spread_rows[k, pl.ds(r, GROUP, stride=SLAB), :] = value
            spread_parts[place, pl.ds(SLAB * part + r, GROUP, stride=POINTS), :] = value
    for i in range(GROUP):
        for place in range(5):
            orbitals[i, :, pl.ds(128 * place, 128)] = spread_parts[
                place, pl.ds(POINTS * i, POINTS), :
            ].astype(jnp.bfloat16)
    for two in range(2):
        for k in range(9):
            value = jnp.concatenate(
                [spread_rows[k + 9 * half, pl.ds(24 * two, 24), :] for half in range(2)], axis=0
            )
            home_in[0, two, :, pl.ds(128 * k, 128)] = value.astype(jnp.bfloat16)
    vis_sum[:, :, pl.ds(32, 16), pl.ds(384, 256)] = jnp.zeros((2, 4, 16, 256), jnp.float32)
    pl.semaphore_wait(barrier, 10)

    def home_copy(source, slot, two, target):
        copy = pltpu.make_async_remote_copy(
            home_in.at[source, two],
            home_in.at[slot, two],
            home_send.at[slot, two],
            home_recv.at[slot, two],
            device_id=target,
        )
        copy.start()
        return copy

    sent = []

    def send_visitors(s):
        for j in range(4):
            copy = pltpu.make_async_remote_copy(
                orbitals.at[j],
                vis_in.at[s, xor(me, j)],
                vis_send.at[s, j],
                vis_recv.at[s, xor(me, j)],
                device_id=(group(BEHIND[s]), j),
            )
            copy.start()
            sent.append(copy)

    sib_copies = [home_copy(0, 1, 0, sibling)]
    send_visitors(0)
    far_copies = [home_copy(0, 2, 0, far)]
    sib_copies.append(home_copy(0, 1, 1, sibling))
    far_copies.append(home_copy(0, 2, 1, far))
    send_visitors(1)

    for load in loads:
        load.start()

    def widen(s, slots):
        for q in slots:
            pltpu.make_async_remote_copy(
                orbitals.at[0], vis_in.at[s, q], vis_send.at[s, 0], vis_recv.at[s, q],
                device_id=sibling,
            ).wait_recv()
            for place in range(5):
                value = vis_in[s, q, :, pl.ds(128 * place, 128)].astype(jnp.float32)
                for part in range(4 if place < 3 else 3):
                    half, k = divmod(5 * part + place, 9)
                    rows = value[SLAB * part : SLAB * part + SLAB]
                    for copy in range(2):
                        wide[s, q, pl.ds(24 * half + SLAB * copy, SLAB), pl.ds(128 * k, 128)] = rows

    def forward(two):
        for cls in range(4):
            first, lanes = CLASSES[cls]
            at = (pl.ds(HALF * two, HALF), pl.ds(first, lanes))
            value = plane(two, cls, (z_hi, z_lo), weights(small, large, 0, cls))
            s_hi[at], s_lo[at] = parted(value)

    def backward(two):
        for cls in range(4):
            first, lanes = CLASSES[cls]
            at = (pl.ds(HALF * two, HALF), pl.ds(first, lanes))
            g[at] = plane(two, cls, (s_hi, s_lo), weights(small, large, 1, cls))

    def across(two):
        for start in range(0, PLANE, 768):
            middle(start, two, (s_hi, s_lo), (s_hi, s_lo), along_x, screened)

    def slab(q, two, s):
        products(q, two, s == 1, home_in, wide.at[s], g, home_sum, vis_part, vis_sum.at[s])

    def send_back(s, q):
        code_visitor(vis_sum.at[s, q], vis_code.at[s, q])
        copy = pltpu.make_async_remote_copy(
            vis_code.at[s, q],
            vis_back.at[s, me],
            back_send.at[s, q],
            back_recv.at[s, me],
            device_id=(group(-BEHIND[s]), xor(me, q)),
        )
        copy.start()
        sent.append(copy)

    def sum_copy(source, target_ref, two, kind, target):
        copy = pltpu.make_async_remote_copy(
            source, target_ref, sum_send.at[two, kind], sum_recv.at[two, kind], device_id=target
        )
        copy.start()
        sent.append(copy)
        return copy

    columns = [pl.ds(128 * k, 128) for k in range(9)]

    def to_far(two, relayed):
        relayed.wait_recv()
        for lanes in columns:
            far_sum[:, lanes] = home_sum[2, two, :, lanes] + sib_relay[two, :, lanes]
        scale = scale_of([far_sum[:, lanes] for lanes in columns])
        for lanes in columns:
            far_out[two, :, lanes] = coded(far_sum[:, lanes], scale)
        far_out[two, :, pl.ds(PLANE // 2, 128)] = jnp.broadcast_to(scale, (POINTS, 128)).astype(jnp.bfloat16)
        return sum_copy(far_out.at[two], far_in.at[two], two, 1, far)

    sib_copies[0].wait_recv()
    widen(0, (0, 1))
    densities(0, 0, home_in, wide.at[0], z_hi, z_lo)
    far_copies[0].wait_recv()
    relays = [home_copy(2, 3, 0, sibling)]
    widen(0, (2, 3))
    relays[0].wait_recv()
    densities(1, 0, home_in, wide.at[0], z_hi, z_lo)
    for load in loads:
        load.wait()
    forward(0)
    across(0)
    backward(0)
    far_copies[1].wait_recv()
    relays.append(home_copy(2, 3, 1, sibling))
    for q in range(4):
        slab(q, 0, 0)

    sib_copies[1].wait_recv()
    densities(0, 1, home_in, wide.at[0], z_hi, z_lo)
    relays[1].wait_recv()
    densities(1, 1, home_in, wide.at[0], z_hi, z_lo)
    forward(1)
    across(1)
    backward(1)
    for q in (2, 3, 0, 1):
        slab(q, 1, 0)
        send_back(0, q)

    widen(1, range(4))
    for pair in range(2):
        densities(pair, 0, home_in, wide.at[1], z_hi, z_lo)
    forward(0)
    across(0)
    backward(0)
    slab(3, 0, 1)
    relayed = sum_copy(home_sum.at[3, 0], sib_relay.at[0], 0, 0, sibling)
    slab(2, 0, 1)
    slab(1, 0, 1)
    finals = [sum_copy(home_sum.at[1, 0], sib_final.at[0], 0, 2, sibling)]
    slab(0, 0, 1)

    for pair in range(2):
        densities(pair, 1, home_in, wide.at[1], z_hi, z_lo)
    fars = [to_far(0, relayed)]
    forward(1)
    across(1)
    backward(1)
    slab(3, 1, 1)
    relayed = sum_copy(home_sum.at[3, 1], sib_relay.at[1], 1, 0, sibling)
    send_back(1, 3)
    slab(2, 1, 1)
    send_back(1, 2)
    fars.append(to_far(1, relayed))
    slab(1, 1, 1)
    finals.append(sum_copy(home_sum.at[1, 1], sib_final.at[1], 1, 2, sibling))
    slab(0, 1, 1)
    send_back(1, 1)
    send_back(1, 0)

    def returned(s):
        for j in range(4):
            pltpu.make_async_remote_copy(
                vis_code.at[s, 0], vis_back.at[s, j], back_send.at[s, 0], back_recv.at[s, j],
                device_id=sibling,
            ).wait_recv()
        return [
            1.0 / vis_back[s, i, pl.ds(32, 16), pl.ds(384, 128)].astype(jnp.float32)[15:] for i in range(4)
        ]

    def far_scale(two):
        return 1.0 / far_in[two, pl.ds(0, 16), pl.ds(PLANE // 2, 128)].astype(jnp.float32)[:1]

    finals[0].wait_recv()
    fars[0].wait_recv()
    inverse = far_scale(0)
    for lanes in columns:
        home_sum[0, 0, :, lanes] = (
            home_sum[0, 0, :, lanes] + sib_final[0, :, lanes] + decoded(far_in[0, :, lanes], inverse)
        )
    inverses = returned(0)
    for i in range(GROUP):
        for place in range(5):
            lanes = pl.ds(128 * place, 128)
            vis_sum[1, i, :, lanes] = decoded(vis_back[0, i, :, lanes], inverses[i])
    finals[1].wait_recv()
    for lanes in columns:
        home_sum[0, 1, :, lanes] = home_sum[0, 1, :, lanes] + sib_final[1, :, lanes]
    inverses = returned(1)
    for i in range(GROUP):
        for place in range(5):
            lanes = pl.ds(128 * place, 128)
            vis_sum[1, i, :, lanes] = vis_sum[1, i, :, lanes] + decoded(vis_back[1, i, :, lanes], inverses[i])
    fars[1].wait_recv()
    inverse = far_scale(1)
    for k in range(9):
        lanes = pl.ds(128 * k, 128)
        totals = [
            home_sum[0, 0, :, lanes],
            home_sum[0, 1, :, lanes] + decoded(far_in[1, :, lanes], inverse),
        ]
        for half in range(2):
            column = k + 9 * half
            part, place = divmod(column, 5)
            for i in range(GROUP):
                row = 24 * half + SLAB * (i % 2)
                back = vis_sum[1, i, pl.ds(SLAB * part, SLAB), pl.ds(128 * place, 128)]
                out[:, i, pl.ds(128 * column, 128)] = totals[i // 2][row : row + SLAB] + back

    for copy in far_copies + sib_copies + relays + sent:
        copy.wait_send()


def solution(mesh):
    small, large, along_x, screened = tables()
    any_space = pl.BlockSpec(memory_space=pl.ANY)
    bf16, f32 = jnp.bfloat16, jnp.float32
    dma = pltpu.SemaphoreType.DMA
    call = pl.pallas_call(
        kernel,
        out_shape=pltpu.VMEM((SLAB, GROUP, PLANE), f32),
        in_specs=[pl.BlockSpec(memory_space=pltpu.VMEM)] + [any_space] * 4,
        out_specs=pl.BlockSpec(memory_space=pltpu.VMEM),
        scratch_shapes=[
            pltpu.VMEM((18, POINTS, 128), f32),
            pltpu.VMEM((5, ROWS, 128), f32),
            pltpu.VMEM((GROUP, POINTS, 640), bf16),
            pltpu.VMEM((4, 2, POINTS, PLANE // 2), bf16),
            pltpu.VMEM((2, 4, POINTS, 640), bf16),
            pltpu.VMEM((2, 4, POINTS, PLANE // 2), f32),
            pltpu.VMEM((ROWS, PLANE), bf16),
            pltpu.VMEM((ROWS, PLANE), bf16),
            pltpu.VMEM((ROWS, PLANE), bf16),
            pltpu.VMEM((ROWS, PLANE), bf16),
            pltpu.VMEM((ROWS, PLANE), f32),
            pltpu.VMEM((4, 2, POINTS, PLANE // 2), f32),
            pltpu.VMEM((4, POINTS, PLANE // 2), f32),
            pltpu.VMEM((2, 4, POINTS, 640), f32),
            pltpu.VMEM((2, 4, POINTS, 640), bf16),
            pltpu.VMEM((2, POINTS, PLANE // 2), f32),
            pltpu.VMEM((2, POINTS, PLANE // 2), f32),
            pltpu.VMEM((POINTS, PLANE // 2), f32),
            pltpu.VMEM((2, POINTS, PLANE // 2 + 128), bf16),
            pltpu.VMEM((2, POINTS, PLANE // 2 + 128), bf16),
            pltpu.VMEM((2, 4, POINTS, 640), bf16),
            pltpu.VMEM(small.shape, bf16),
            pltpu.VMEM(large.shape, bf16),
            pltpu.VMEM(along_x.shape[1:], bf16),
            pltpu.VMEM(screened.shape, f32),
            dma((4,)), dma((4, 2)), dma((4, 2)), dma((2, 4)), dma((2, 4)),
            dma((2, 3)), dma((2, 3)), dma((2, 4)), dma((2, 4)),
        ],
        compiler_params=pltpu.CompilerParams(
            collective_id=0, has_side_effects=True, vmem_limit_bytes=60 << 20
        ),
    )

    def body(orbitals):
        return -MIXING * jnp.transpose(
            call(jnp.transpose(orbitals, (1, 0, 2)), small, large, along_x, screened), (1, 0, 2)
        )

    placed = P("band", "grid", None)
    return jax.shard_map(
        body, mesh=mesh, in_specs=(placed,), out_specs=placed, check_vma=False
    )
```

time: 53.1 us -> 46.9 us (0.88)
  the two profiles are of different devices: /device:TPU:1 before, /device:TPU:11 now
where the time goes in v2:
time: 46.9 us; the launch traced here: 46.8 us
  Pallas kernels  45.9 us (98%)
  other arithmetic  0.86 us (2%)
    pallas_call x1, Pallas kernels, body(): call(jnp.transpose(orbitals, (1, 0, 2)), small, large, along_x, screened)  45.9 us

profile of v2, /device:TPU:11, one launch (start us, length us, event | category | flops | bytes accessed | tf_op | source)
XLA Modules:
  0.0 46.8 jit_solution(2006636025842117433)
XLA Ops:
  0.0 45.9 %shard_map.55 = f32[12,4,2304]{2,1,0:T(4,128)S(1)} custom-call(bf16[12,4,2304]{2,1,0:T(4,128)(2,1)} %bitcast.3, bf16[2,4,384,384]{3,2,1,0:T(8,128)(2,1)} %constant.10.clone.small_hbm, bf16[2,4,768,768]{3,2,1,0:T(8,128)(2,1)} %constant.11.clone.large_hbm, bf16[4,2,192,192]{3,2,1,0:T(8,128)(2,1)} %constant.12.clone.along_hbm, ...), custom_call_target="tpu_custom_call" | custom-call | tf_op jit(solution)/shard_map/pallas_call | solution.py:520
  45.9 0.9 %multiply_bitcast_fusion = f32[4,12,2304]{2,0,1:T(4,128)} fusion(f32[12,4,2304]{2,1,0:T(4,128)S(1)} %shard_map.55), kind=kLoop, calls=%fused_computation | loop fusion | flops 110592 | bytes 884736 | tf_op jit(solution)/shard_map/mul | solution.py:519

commit v3 on v2

--- a/solution.py
+++ b/solution.py
@@ -268,26 +268,32 @@
         copy.start()
         return copy
 
-    sent = []
-
-    def send_visitors(s):
-        for j in range(4):
-            copy = pltpu.make_async_remote_copy(
+    visits = [
+        [
+            pltpu.make_async_remote_copy(
                 orbitals.at[j],
                 vis_in.at[s, xor(me, j)],
                 vis_send.at[s, j],
                 vis_recv.at[s, xor(me, j)],
                 device_id=(group(BEHIND[s]), j),
             )
+            for j in range(4)
+        ]
+        for s in range(2)
+    ]
+    sent = visits[0] + visits[1]
+
+    def send_visitors(s):
+        for copy in visits[s]:
             copy.start()
-            sent.append(copy)
-
+
+    turn = lax.rem(band // 2, 8) == 7
     sib_copies = [home_copy(0, 1, 0, sibling)]
     send_visitors(0)
+    pl.when(turn)(functools.partial(send_visitors, 1))
     far_copies = [home_copy(0, 2, 0, far)]
     sib_copies.append(home_copy(0, 1, 1, sibling))
     far_copies.append(home_copy(0, 2, 1, far))
-    send_visitors(1)
 
     for load in loads:
         load.start()
@@ -363,6 +369,7 @@
     densities(0, 0, home_in, wide.at[0], z_hi, z_lo)
     far_copies[0].wait_recv()
     relays = [home_copy(2, 3, 0, sibling)]
+    pl.when(jnp.logical_not(turn))(functools.partial(send_visitors, 1))
     widen(0, (2, 3))
     relays[0].wait_recv()
     densities(1, 0, home_in, wide.at[0], z_hi, z_lo)

time: 46.9 us -> 47.6 us (1.015)
  the two profiles are of different devices: /device:TPU:11 before, /device:TPU:1 now
where the time goes in v3:
time: 47.6 us; the launch traced here: 47.5 us
  Pallas kernels  46.7 us (98%)
  other arithmetic  0.86 us (2%)
    pallas_call x1, Pallas kernels, body(): call(jnp.transpose(orbitals, (1, 0, 2)), small, large, along_x, screened)  46.7 us

profile of v3, /device:TPU:1, one launch (start us, length us, event | category | flops | bytes accessed | tf_op | source)
XLA Modules:
  0.0 47.5 jit_solution(10690128818628028909)
XLA Ops:
  0.0 46.7 %shard_map.55 = f32[12,4,2304]{2,1,0:T(4,128)S(1)} custom-call(bf16[12,4,2304]{2,1,0:T(4,128)(2,1)} %bitcast.3, bf16[2,4,384,384]{3,2,1,0:T(8,128)(2,1)} %constant.10.clone.small_hbm, bf16[2,4,768,768]{3,2,1,0:T(8,128)(2,1)} %constant.11.clone.large_hbm, bf16[4,2,192,192]{3,2,1,0:T(8,128)(2,1)} %constant.12.clone.along_hbm, ...), custom_call_target="tpu_custom_call" | custom-call | tf_op jit(solution)/shard_map/pallas_call | solution.py:527
  46.7 0.9 %multiply_bitcast_fusion = f32[4,12,2304]{2,0,1:T(4,128)} fusion(f32[12,4,2304]{2,1,0:T(4,128)S(1)} %shard_map.55), kind=kLoop, calls=%fused_computation | loop fusion | flops 110592 | bytes 884736 | tf_op jit(solution)/shard_map/mul | solution.py:526

commit v4 on v2

--- a/solution.py
+++ b/solution.py
@@ -201,8 +201,8 @@
 
 
 def kernel(
-    arrived, small_hbm, large_hbm, along_hbm, screened_hbm, out,
-    spread_rows, spread_parts, orbitals, home_in, vis_in, wide, z_hi, z_lo, s_hi, s_lo, g,
+    arrived_hbm, small_hbm, large_hbm, along_hbm, screened_hbm, out,
+    arrived, spread_rows, spread_parts, orbitals, home_in, vis_in, wide, z_hi, z_lo, s_hi, s_lo, g,
     home_sum, vis_part, vis_sum, vis_code, sib_relay, sib_final, far_sum, far_out, far_in, vis_back,
     small, large, along_x, screened,
     table_sem, home_send, home_recv, vis_send, vis_recv,
@@ -230,6 +230,8 @@
         for j in range(4):
             pl.semaphore_signal(barrier, 1, device_id=(group(-distance), j))
 
+    entry = pltpu.make_async_copy(arrived_hbm, arrived, table_sem.at[4])
+    entry.start()
     loads = [
         pltpu.make_async_copy(small_hbm, small, table_sem.at[0]),
         pltpu.make_async_copy(large_hbm, large, table_sem.at[1]),
@@ -237,6 +239,7 @@
         pltpu.make_async_copy(screened_hbm, screened, table_sem.at[3]),
     ]
     spread_parts[3:5] = jnp.zeros((2, ROWS, 128), jnp.float32)
+    entry.wait()
     for k in range(18):
         part, place = divmod(k, 5)
         for r in range(SLAB):
@@ -479,9 +482,10 @@
     call = pl.pallas_call(
         kernel,
         out_shape=pltpu.VMEM((SLAB, GROUP, PLANE), f32),
-        in_specs=[pl.BlockSpec(memory_space=pltpu.VMEM)] + [any_space] * 4,
+        in_specs=[any_space] * 5,
         out_specs=pl.BlockSpec(memory_space=pltpu.VMEM),
         scratch_shapes=[
+            pltpu.VMEM((SLAB, GROUP, PLANE), bf16),
             pltpu.VMEM((18, POINTS, 128), f32),
             pltpu.VMEM((5, ROWS, 128), f32),
             pltpu.VMEM((GROUP, POINTS, 640), bf16),
@@ -507,7 +511,7 @@
             pltpu.VMEM(large.shape, bf16),
             pltpu.VMEM(along_x.shape[1:], bf16),
             pltpu.VMEM(screened.shape, f32),
-            dma((4,)), dma((4, 2)), dma((4, 2)), dma((2, 4)), dma((2, 4)),
+            dma((5,)), dma((4, 2)), dma((4, 2)), dma((2, 4)), dma((2, 4)),
             dma((2, 3)), dma((2, 3)), dma((2, 4)), dma((2, 4)),
         ],
         compiler_params=pltpu.CompilerParams(

time: 46.9 us -> 46 us (0.981)
  Pallas kernels: 45.9 us -> 45 us
    pallas_call x1, Pallas kernels: 45.9 us -> 45 us  [body(): call(jnp.transpose(orbitals, (1, 0, 2)), small, large, along_x, screened)]
where the time goes in v4:
time: 46 us; the launch traced here: 45.9 us
  Pallas kernels  45 us (98%)
  other arithmetic  0.86 us (2%)
    pallas_call x1, Pallas kernels, body(): call(jnp.transpose(orbitals, (1, 0, 2)), small, large, along_x, screened)  45 us

profile of v4, /device:TPU:11, one launch (start us, length us, event | category | flops | bytes accessed | tf_op | source)
XLA Modules:
  0.0 45.9 jit_solution(7243270937414239927)
XLA Ops:
  0.0 45.0 %shard_map.55 = f32[12,4,2304]{2,1,0:T(4,128)S(1)} custom-call(bf16[12,4,2304]{2,1,0:T(4,128)(2,1)} %bitcast.3, bf16[2,4,384,384]{3,2,1,0:T(8,128)(2,1)} %constant.10.clone.small_hbm, bf16[2,4,768,768]{3,2,1,0:T(8,128)(2,1)} %constant.11.clone.large_hbm, bf16[4,2,192,192]{3,2,1,0:T(8,128)(2,1)} %constant.12.clone.along_hbm, ...), custom_call_target="tpu_custom_call" | custom-call | tf_op jit(solution)/shard_map/pallas_call | solution.py:524
  45.0 0.9 %multiply_bitcast_fusion = f32[4,12,2304]{2,0,1:T(4,128)} fusion(f32[12,4,2304]{2,1,0:T(4,128)S(1)} %shard_map.55), kind=kLoop, calls=%fused_computation | loop fusion | flops 110592 | bytes 884736 | tf_op jit(solution)/shard_map/mul | solution.py:523
